TPU v7x, 32 devices: a whole 2x2x4 slice. The times are simulated.
32 devices in a mesh: ctx: 16 (over z, x, core), chan: 2 (over y).
Axes of the slice: x: 2, y: 2, z: 4, core: 2. Of those that a mesh axis runs over, the one named last changes fastest.
Arguments:
- grad_out: bfloat16 [64, 16384], P('chan', 'ctx'), may hold values from -6 to 6
- query: bfloat16 [64, 16384], P('chan', 'ctx'), may hold values from -6 to 6
- key_proj: bfloat16 [64, 16384], P('chan', 'ctx'), may hold values from -6 to 6
- value: bfloat16 [64, 16384], P('chan', 'ctx'), may hold values from -6 to 6
- filter_param: float32 [32, 16384], P(None, 'ctx'), may hold values from -6 to 6
Outputs:
- grad_query: bfloat16 [64, 16384], P('chan', 'ctx')
- grad_key: bfloat16 [64, 16384], P('chan', 'ctx')
- grad_value: bfloat16 [64, 16384], P('chan', 'ctx')
- grad_filter: float32 [32, 16384], P(None, 'ctx')
All inputs are finite; a program needn't handle non-finite values.
Results may differ from a plain program's by a relative error of at most 0.004.
Values sent between devices are 32-bit elements; how exact they have to be, the bound alone decides.
A program may use at most 128 MiB of HBM per device.

v0:
```python
import functools
import math

import jax
import jax.numpy as jnp
from jax import lax
from jax.experimental import pallas as pl
from jax.experimental.pallas import tpu as pltpu
from jax.sharding import PartitionSpec as P

LANES = 128
STEPS = 16
DEPTH = STEPS * LANES
F32 = jnp.float32
BF16 = jnp.bfloat16


def rows_at(ref, start, count):
    return ref.at[pl.ds(pl.multiple_of(start, 8), count), :]


def split_rows(values, stage, tiles):
    for k in range(tiles):
        stage[pl.ds(k, values.shape[0], stride=tiles), :] = values[:, k * LANES : (k + 1) * LANES]


def convolve_kernel(n_ctx, n_merge, scale, go_ref, q_ref, k_ref, v_ref, f_ref, landed_ref,
                    f_stage, s_stage, c_stage, f_land, s_land, c_land, c_pad, s_lhs, c_lhs, toep,
                    conv, back, corr, send_sem, recv_sem, own_sem):
    tiles = go_ref.shape[1] // LANES
    blocks = n_ctx * tiles
    span = blocks + STEPS
    peers = n_ctx * n_merge
    my_ctx = lax.axis_index("ctx")
    my_chan = lax.axis_index("chan") if n_merge > 1 else 0
    me = my_ctx * n_merge + my_chan

    offsets = [(c, j) for c in range(n_ctx) for j in range(n_merge) if (c, j) != (0, 0)]
    offsets.sort(key=lambda o: (abs(o[0] - n_ctx // 2), o))
    others = []
    for c, j in offsets:
        ctx = (my_ctx + c) % n_ctx
        chan = (my_chan + j) % n_merge if n_merge > 1 else 0
        ident = {"ctx": ctx, "chan": chan} if n_merge > 1 else {"ctx": ctx}
        others.append((j == 0, ctx, chan, ctx * n_merge + chan, ident))

    barrier = pltpu.get_barrier_semaphore()
    for _, _, _, _, ident in others:
        pl.semaphore_signal(barrier, inc=1, device_id=ident, device_id_type=pl.DeviceIdType.MESH)

    def remote(src, dst, n, ident):
        return pltpu.make_async_remote_copy(
            src_ref=src, dst_ref=dst, send_sem=send_sem.at[n], recv_sem=recv_sem.at[n],
            device_id=ident, device_id_type=pl.DeviceIdType.MESH,
        )

    def whole(stage, n, count):
        part = stage.at[pl.ds(0, count * tiles), :]
        return remote(part, part, n, others[0][4])

    split_rows(f_ref[...] * scale, f_stage, tiles)
    split_rows(k_ref[...].astype(F32) * v_ref[...].astype(F32), s_stage, tiles)
    pl.semaphore_wait(barrier, peers - 1)
    for same, ctx, chan, peer, ident in others:
        if same:
            remote(rows_at(f_stage, peer * tiles, tiles), rows_at(f_land, my_ctx * tiles, tiles), 0, ident).start()
    for _, ctx, chan, peer, ident in others:
        remote(
            rows_at(s_stage, peer * tiles, tiles),
            rows_at(s_land, my_chan * span + STEPS + my_ctx * tiles, tiles), 1, ident,
        ).start()
    split_rows(go_ref[...].astype(F32) * q_ref[...].astype(F32), c_stage, tiles)
    for _, ctx, chan, peer, ident in others:
        remote(
            rows_at(c_stage, peer * tiles, tiles),
            rows_at(c_land, my_chan * blocks + my_ctx * tiles, tiles), 2, ident,
        ).start()
    mine = pl.ds(pl.multiple_of(me * tiles, 8), tiles)
    f_land[pl.ds(pl.multiple_of(my_ctx * tiles, 8), tiles), :] = f_stage[mine, :]
    s_land[pl.ds(pl.multiple_of(my_chan * span + STEPS + my_ctx * tiles, 8), tiles), :] = s_stage[mine, :]
    c_land[pl.ds(pl.multiple_of(my_chan * blocks + my_ctx * tiles, 8), tiles), :] = c_stage[mine, :]
    for ch in range(n_merge):
        s_land[ch * span : ch * span + STEPS, :] = jnp.zeros((STEPS, LANES), F32)
        c_pad[ch * span + blocks : (ch + 1) * span, :] = jnp.zeros((STEPS, LANES), F32)

    lane = lax.broadcasted_iota(jnp.int32, (LANES, LANES), 1)
    row = lax.broadcasted_iota(jnp.int32, (LANES, LANES), 0)
    flip = (lane + row == LANES - 1).astype(F32)
    current = lane < LANES - row

    def reverse(values):
        return jnp.dot(values, flip, precision=lax.Precision.HIGHEST, preferred_element_type=F32)

    def skew(before, now):
        picked = jnp.where(
            current, jnp.broadcast_to(now, (LANES, LANES)), jnp.broadcast_to(before, (LANES, LANES))
        )
        return pltpu.roll(picked, 0, 1, stride=1, stride_axis=0).astype(BF16)

    whole(f_stage, 0, n_ctx - 1).wait_recv()

    def build(src, before):
        rows = f_land[pl.ds(pl.multiple_of(src * tiles, 8), tiles), :]
        for k in range(tiles):
            now = rows[k : k + 1, :]
            toep[0, pl.ds(pl.multiple_of((src * tiles + k) * LANES, LANES), LANES), :] = skew(before, now)
            before = now
        return before

    lax.fori_loop(0, n_ctx, build, jnp.zeros((1, LANES), F32))
    whole(s_stage, 1, peers - 1).wait_recv()
    for ch in range(n_merge):
        for dd in range(STEPS):
            at = ch * span + STEPS - dd
            s_lhs[ch, :, dd * LANES : (dd + 1) * LANES] = s_land[at : at + blocks, :].astype(BF16)

    def band(n, g):
        return toep[n, g * DEPTH : (g + 1) * DEPTH, :]

    for g in range(blocks // STEPS):
        n = blocks - g * STEPS
        lhs = jnp.concatenate([s_lhs[ch, 0:n, :] for ch in range(n_merge)], axis=0)
        prod = jnp.dot(lhs, band(0, g), preferred_element_type=F32)
        for ch in range(n_merge):
            part = prod[ch * n : (ch + 1) * n]
            rows = slice(ch * blocks + g * STEPS, (ch + 1) * blocks)
            conv[rows, :] = part if g == 0 else conv[rows, :] + part
            for block in range(g * STEPS, (g + 1) * STEPS):
                at = ch * span + STEPS + block
                toep[1 + ch, block * LANES : (block + 1) * LANES, :] = skew(
                    s_land[at - 1 : at, :], s_land[at : at + 1, :]
                )

    def send_result(src_of, a):
        for _, ctx, chan, peer, ident in others:
            remote(src_of(ctx, chan), rows_at(landed_ref, (me * 3 + a) * tiles, tiles), 3 + a, ident).start()
        own = pltpu.make_async_copy(
            src_of(my_ctx, my_chan), rows_at(landed_ref, (me * 3 + a) * tiles, tiles), own_sem.at[a]
        )
        own.start()
        return own

    owns = [send_result(lambda ctx, chan: rows_at(conv, chan * blocks + ctx * tiles, tiles), 0)]

    whole(c_stage, 2, peers - 1).wait_recv()
    for ch in range(n_merge):
        c_pad[ch * span : ch * span + blocks, :] = reverse(c_land[ch * blocks : (ch + 1) * blocks, :])
        for dd in range(STEPS):
            at = ch * span + dd
            c_lhs[ch, :, dd * LANES : (dd + 1) * LANES] = c_pad[at : at + blocks, :].astype(BF16)

    for g in range(blocks // STEPS):
        n = blocks - g * STEPS
        lhs = jnp.concatenate([c_lhs[ch, g * STEPS : blocks, :] for ch in range(n_merge)], axis=0)
        prod = jnp.dot(lhs, band(0, g), preferred_element_type=F32)
        for ch in range(n_merge):
            part = prod[ch * n : (ch + 1) * n]
            rows = slice(ch * blocks, ch * blocks + n)
            back[rows, :] = part if g == 0 else back[rows, :] + part
    back[...] = reverse(back[...])
    owns.append(send_result(lambda ctx, chan: rows_at(back, chan * blocks + ctx * tiles, tiles), 1))

    for g in range(blocks // STEPS):
        n = blocks - g * STEPS
        for ch in range(n_merge):
            part = jnp.dot(c_lhs[ch, g * STEPS : blocks, :], band(1 + ch, g), preferred_element_type=F32)
            corr[0:n, :] = part if g == 0 and ch == 0 else corr[0:n, :] + part
    corr[...] = reverse(corr[...]) * scale
    owns.append(send_result(lambda ctx, chan: rows_at(corr, ctx * tiles, tiles), 2))

    whole(f_stage, 0, n_ctx - 1).wait_send()
    whole(s_stage, 1, peers - 1).wait_send()
    whole(c_stage, 2, peers - 1).wait_send()
    for a in range(3):
        owns[a].wait()
        whole(s_stage, 3 + a, peers - 1).wait_send()
        whole(s_stage, 3 + a, peers - 1).wait_recv()


def gate_kernel(go_ref, k_ref, v_ref, landed_ref, dq_ref, dk_ref, dv_ref, df_ref):
    rows, width = go_ref.shape
    tiles = width // LANES
    size = 3 * tiles
    for k in range(tiles):
        cols = slice(k * LANES, (k + 1) * LANES)
        conv = landed_ref[pl.ds(k, rows, stride=size), :]
        back = landed_ref[pl.ds(tiles + k, rows, stride=size), :]
        dq_ref[:, cols] = (go_ref[:, cols].astype(F32) * conv).astype(BF16)
        dk_ref[:, cols] = (back * v_ref[:, cols].astype(F32)).astype(BF16)
        dv_ref[:, cols] = (back * k_ref[:, cols].astype(F32)).astype(BF16)
        df_ref[:, cols] = landed_ref[pl.ds(2 * tiles + k, rows, stride=size), :]


def vmem(count):
    return [pl.BlockSpec(memory_space=pltpu.VMEM)] * count


def local(grad_out, query, key_proj, value, filter_param):
    n_ctx = lax.axis_size("ctx")
    n_chan = lax.axis_size("chan")
    rows, width = grad_out.shape
    tiles = width // LANES
    n_merge = n_chan if rows == n_ctx * n_chan else 1
    peers = n_ctx * n_merge
    blocks = n_ctx * tiles
    if rows != peers or filter_param.shape[0] != rows or tiles % 8 or blocks % STEPS:
        raise ValueError("unsupported sizes")
    scale = 1.0 / math.sqrt(n_ctx * width)
    span = blocks + STEPS
    dma = pltpu.SemaphoreType.DMA

    def buffer(*shape, dtype=F32):
        return pltpu.VMEM(shape, dtype)

    landed = pl.pallas_call(
        functools.partial(convolve_kernel, n_ctx, n_merge, scale),
        out_shape=jax.ShapeDtypeStruct((peers * 3 * tiles, LANES), F32),
        in_specs=vmem(5),
        out_specs=pl.BlockSpec(memory_space=pl.ANY),
        scratch_shapes=[
            buffer(rows * tiles, LANES),
            buffer(rows * tiles, LANES),
            buffer(rows * tiles, LANES),
            buffer(blocks, LANES),
            buffer(n_merge * span, LANES),
            buffer(n_merge * blocks, LANES),
            buffer(n_merge * span, LANES),
            buffer(n_merge, blocks, DEPTH, dtype=BF16),
            buffer(n_merge, blocks, DEPTH, dtype=BF16),
            buffer(1 + n_merge, blocks * LANES, LANES, dtype=BF16),
            buffer(n_merge * blocks, LANES),
            buffer(n_merge * blocks, LANES),
            buffer(blocks, LANES),
            dma((6,)),
            dma((6,)),
            dma((3,)),
        ],
        compiler_params=pltpu.CompilerParams(
            collective_id=0, has_side_effects=True, vmem_limit_bytes=48 * 1024 * 1024
        ),
        name="long_convolutions",
    )(grad_out, query, key_proj, value, filter_param)
    dq, dk, dv, df = pl.pallas_call(
        gate_kernel,
        out_shape=(
            jax.ShapeDtypeStruct((rows, width), BF16),
            jax.ShapeDtypeStruct((rows, width), BF16),
            jax.ShapeDtypeStruct((rows, width), BF16),
            jax.ShapeDtypeStruct((rows, width), F32),
        ),
        in_specs=vmem(4),
        out_specs=tuple(vmem(4)),
        name="gate_gradients",
    )(grad_out, key_proj, value, landed)
    if n_merge == 1:
        df = lax.psum(df, "chan")
    return (dq, dk, dv, df)


def solution(mesh):
    in_specs = (
        P("chan", "ctx"),
        P("chan", "ctx"),
        P("chan", "ctx"),
        P("chan", "ctx"),
        P(None, "ctx"),
    )
    out_specs = (P("chan", "ctx"), P("chan", "ctx"), P("chan", "ctx"), P(None, "ctx"))
    return jax.shard_map(local, mesh=mesh, in_specs=in_specs, out_specs=out_specs, check_vma=False)
```

profile of v0, /device:TPU:0, one launch (start us, length us, event | category | flops | bytes accessed | tf_op | source)
XLA Modules:
  0.0 36.1 jit_solution(13475470122682363023)
XLA Ops:
  0.6 0.0 copy-start.1
  0.6 0.8 %copy-done.1 = bf16[32,1024]{1,0:T(8,128)(2,1)S(1)} copy-done((bf16[32,1024]{1,0:T(8,128)(2,1)S(1)}, bf16[32,1024]{1,0:T(8,128)(2,1)}, u32[]{:S(2)}) %copy-start.1) | copy-done | bytes 65560
  1.5 0.0 copy-start.2
  1.5 0.8 %copy-done.2 = bf16[32,1024]{1,0:T(8,128)(2,1)S(1)} copy-done((bf16[32,1024]{1,0:T(8,128)(2,1)S(1)}, bf16[32,1024]{1,0:T(8,128)(2,1)}, u32[]{:S(2)}) %copy-start.2) | copy-done | bytes 65560
  2.3 0.0 copy-start.3
  2.3 0.8 %copy-done.3 = bf16[32,1024]{1,0:T(8,128)(2,1)S(1)} copy-done((bf16[32,1024]{1,0:T(8,128)(2,1)S(1)}, bf16[32,1024]{1,0:T(8,128)(2,1)}, u32[]{:S(2)}) %copy-start.3) | copy-done | bytes 65560
  3.2 0.0 copy-start.4
  3.2 0.9 %copy-done.4 = f32[32,1024]{1,0:T(8,128)S(1)} copy-done((f32[32,1024]{1,0:T(8,128)S(1)}, f32[32,1024]{1,0:T(8,128)}, u32[]{:S(2)}) %copy-start.4) | copy-done | bytes 131096
  4.1 0.0 copy-start.5
  4.1 0.8 %copy-done.5 = bf16[32,1024]{1,0:T(8,128)(2,1)S(1)} copy-done((bf16[32,1024]{1,0:T(8,128)(2,1)S(1)}, bf16[32,1024]{1,0:T(8,128)(2,1)}, u32[]{:S(2)}) %copy-start.5) | copy-done | bytes 65560
  4.9 28.6 %long_convolutions.1.landed_ref = f32[768,128]{1,0:T(8,128)S(1)} custom-call(bf16[32,1024]{1,0:T(8,128)(2,1)S(1)} %copy-done.1, bf16[32,1024]{1,0:T(8,128)(2,1)S(1)} %copy-done.5, bf16[32,1024]{1,0:T(8,128)(2,1)S(1)} %copy-done.2, bf16[32,1024]{1,0:T(8,128)(2,1)S(1)} %copy-done.3, f32[32,1024]{1,0:T(8,128)S(1)} %copy-done.4), custom_call_target="tpu_custom_call" | custom-call | tf_op jit(solution)/shard_map/long_convolutions/pallas_call | solution.py:215
  33.5 0.0 copy-start
  33.5 0.7 %copy-done = f32[768,128]{1,0:T(8,128)} copy-done((f32[768,128]{1,0:T(8,128)}, f32[768,128]{1,0:T(8,128)S(1)}, u32[]{:S(2)}) %copy-start) | copy-done | bytes 393240
  34.2 1.9 %gate_gradients.1 = (bf16[32,1024]{1,0:T(8,128)(2,1)}, bf16[32,1024]{1,0:T(8,128)(2,1)}, bf16[32,1024]{1,0:T(8,128)(2,1)}, f32[32,1024]{1,0:T(8,128)}) custom-call(bf16[32,1024]{1,0:T(8,128)(2,1)} %go_ref.3, bf16[32,1024]{1,0:T(8,128)(2,1)} %k_ref.3, bf16[32,1024]{1,0:T(8,128)(2,1)} %v_ref.3, f32[768,128]{1,0:T(8,128)} %copy-done), custom_call_target="tpu_custom_call" | custom-call | tf_op jit(solution)/shard_map/gate_gradients/pallas_call | solution.py:243
Async XLA Ops:
  0.6 0.8 %copy-start.1 = (bf16[32,1024]{1,0:T(8,128)(2,1)S(1)}, bf16[32,1024]{1,0:T(8,128)(2,1)}, u32[]{:S(2)}) copy-start(bf16[32,1024]{1,0:T(8,128)(2,1)} %go_ref.3) | copy-start | bytes 196612
  1.5 0.8 %copy-start.2 = (bf16[32,1024]{1,0:T(8,128)(2,1)S(1)}, bf16[32,1024]{1,0:T(8,128)(2,1)}, u32[]{:S(2)}) copy-start(bf16[32,1024]{1,0:T(8,128)(2,1)} %k_ref.3) | copy-start | bytes 196612
  2.3 0.8 %copy-start.3 = (bf16[32,1024]{1,0:T(8,128)(2,1)S(1)}, bf16[32,1024]{1,0:T(8,128)(2,1)}, u32[]{:S(2)}) copy-start(bf16[32,1024]{1,0:T(8,128)(2,1)} %v_ref.3) | copy-start | bytes 196612
  3.2 0.9 %copy-start.4 = (f32[32,1024]{1,0:T(8,128)S(1)}, f32[32,1024]{1,0:T(8,128)}, u32[]{:S(2)}) copy-start(f32[32,1024]{1,0:T(8,128)} %f_ref.1) | copy-start | bytes 393220
  4.1 0.8 %copy-start.5 = (bf16[32,1024]{1,0:T(8,128)(2,1)S(1)}, bf16[32,1024]{1,0:T(8,128)(2,1)}, u32[]{:S(2)}) copy-start(bf16[32,1024]{1,0:T(8,128)(2,1)} %q_ref.1) | copy-start | bytes 196612
  33.5 0.7 %copy-start = (f32[768,128]{1,0:T(8,128)}, f32[768,128]{1,0:T(8,128)S(1)}, u32[]{:S(2)}) copy-start(f32[768,128]{1,0:T(8,128)S(1)} %long_convolutions.1.landed_ref) | copy-start | bytes 1179652
where the time goes:
time: 36.4 us; the launch traced here: 36.1 us
  Pallas kernels  30.5 us (84%)
  local copies, waits for them, and re-layouts  4.99 us (14%)
  between operations  0.66 us (2%)
    pallas_call x1, Pallas kernels, local(): pl.pallas_call(functools.partial(convolve_kernel, n_ctx, n_merge, scale),...  28.6 us
    unnamed x12, local copies, waits for them, and re-layouts  4.99 us
    pallas_call x1, Pallas kernels, local(): pl.pallas_call(gate_kernel, out_shape=(jax.ShapeDtypeStruct((rows, width)...  1.9 us

commit v1 on v0

--- a/solution.py
+++ b/solution.py
@@ -10,6 +10,7 @@
 
 LANES = 128
 STEPS = 16
+VMEM_BYTES = 60 * 1024 * 1024
 DEPTH = STEPS * LANES
 F32 = jnp.float32
 BF16 = jnp.bfloat16
@@ -24,9 +25,17 @@
         stage[pl.ds(k, values.shape[0], stride=tiles), :] = values[:, k * LANES : (k + 1) * LANES]
 
 
-def convolve_kernel(n_ctx, n_merge, scale, go_ref, q_ref, k_ref, v_ref, f_ref, landed_ref,
-                    f_stage, s_stage, c_stage, f_land, s_land, c_land, c_pad, s_lhs, c_lhs, toep,
+def convolve_kernel(n_ctx, n_merge, scale, go_hbm, q_hbm, k_hbm, v_hbm, f_hbm, landed_ref,
+                    go_ref, q_ref, k_ref, v_ref, f_ref, load_sem, f_stage, s_stage, c_stage, f_land, s_land, c_land, c_pad, s_lhs, c_lhs, toep,
                     conv, back, corr, send_sem, recv_sem, own_sem):
+    loads = [
+        pltpu.make_async_copy(src, dst, load_sem.at[n])
+        for n, (src, dst) in enumerate(
+            [(f_hbm, f_ref), (k_hbm, k_ref), (v_hbm, v_ref), (go_hbm, go_ref), (q_hbm, q_ref)]
+        )
+    ]
+    for load in loads:
+        load.start()
     tiles = go_ref.shape[1] // LANES
     blocks = n_ctx * tiles
     span = blocks + STEPS
@@ -58,7 +67,10 @@
         part = stage.at[pl.ds(0, count * tiles), :]
         return remote(part, part, n, others[0][4])
 
+    loads[0].wait()
     split_rows(f_ref[...] * scale, f_stage, tiles)
+    loads[1].wait()
+    loads[2].wait()
     split_rows(k_ref[...].astype(F32) * v_ref[...].astype(F32), s_stage, tiles)
     pl.semaphore_wait(barrier, peers - 1)
     for same, ctx, chan, peer, ident in others:
@@ -69,6 +81,8 @@
             rows_at(s_stage, peer * tiles, tiles),
             rows_at(s_land, my_chan * span + STEPS + my_ctx * tiles, tiles), 1, ident,
         ).start()
+    loads[3].wait()
+    loads[4].wait()
     split_rows(go_ref[...].astype(F32) * q_ref[...].astype(F32), c_stage, tiles)
     for _, ctx, chan, peer, ident in others:
         remote(
@@ -215,9 +229,15 @@
     landed = pl.pallas_call(
         functools.partial(convolve_kernel, n_ctx, n_merge, scale),
         out_shape=jax.ShapeDtypeStruct((peers * 3 * tiles, LANES), F32),
-        in_specs=vmem(5),
+        in_specs=[pl.BlockSpec(memory_space=pl.ANY)] * 5,
         out_specs=pl.BlockSpec(memory_space=pl.ANY),
         scratch_shapes=[
+            buffer(rows, width, dtype=BF16),
+            buffer(rows, width, dtype=BF16),
+            buffer(rows, width, dtype=BF16),
+            buffer(rows, width, dtype=BF16),
+            buffer(rows, width),
+            dma((5,)),
             buffer(rows * tiles, LANES),
             buffer(rows * tiles, LANES),
             buffer(rows * tiles, LANES),
@@ -236,7 +256,7 @@
             dma((3,)),
         ],
         compiler_params=pltpu.CompilerParams(
-            collective_id=0, has_side_effects=True, vmem_limit_bytes=48 * 1024 * 1024
+            collective_id=0, has_side_effects=True, vmem_limit_bytes=VMEM_BYTES
         ),
         name="long_convolutions",
     )(grad_out, query, key_proj, value, filter_param)
@@ -250,6 +270,7 @@
         ),
         in_specs=vmem(4),
         out_specs=tuple(vmem(4)),
+        compiler_params=pltpu.CompilerParams(vmem_limit_bytes=VMEM_BYTES),
         name="gate_gradients",
     )(grad_out, key_proj, value, landed)
     if n_merge == 1:

time: 36.4 us -> 31.5 us (0.87)
  local copies, waits for them, and re-layouts: 4.99 us -> 0 us
    unnamed x12 -> x0, local copies, waits for them, and re-layouts: 4.99 us -> none
where the time goes in v1:
time: 31.5 us; the launch traced here: 31.4 us
  Pallas kernels  30.7 us (97%)
  between operations  0.64 us (2%)
    pallas_call x1, Pallas kernels, local(): pl.pallas_call(functools.partial(convolve_kernel, n_ctx, n_merge, scale),...  28.8 us
    pallas_call x1, Pallas kernels, local(): pl.pallas_call(gate_kernel, out_shape=(jax.ShapeDtypeStruct((rows, width)...  1.9 us

profile of v1, /device:TPU:0, one launch (start us, length us, event | category | flops | bytes accessed | tf_op | source)
XLA Modules:
  0.0 31.4 jit_solution(15969299376532243964)
XLA Ops:
  0.6 28.8 %long_convolutions.1.landed_ref = f32[768,128]{1,0:T(8,128)} custom-call(bf16[32,1024]{1,0:T(8,128)(2,1)} %go_ref.1, bf16[32,1024]{1,0:T(8,128)(2,1)} %q_hbm.1, bf16[32,1024]{1,0:T(8,128)(2,1)} %k_ref.1, bf16[32,1024]{1,0:T(8,128)(2,1)} %v_ref.1, f32[32,1024]{1,0:T(8,128)} %f_hbm.1), custom_call_target="tpu_custom_call" | custom-call | tf_op jit(solution)/shard_map/long_convolutions/pallas_call | solution.py:229
  29.5 1.9 %gate_gradients.1 = (bf16[32,1024]{1,0:T(8,128)(2,1)}, bf16[32,1024]{1,0:T(8,128)(2,1)}, bf16[32,1024]{1,0:T(8,128)(2,1)}, f32[32,1024]{1,0:T(8,128)}) custom-call(bf16[32,1024]{1,0:T(8,128)(2,1)} %go_ref.1, bf16[32,1024]{1,0:T(8,128)(2,1)} %k_ref.1, bf16[32,1024]{1,0:T(8,128)(2,1)} %v_ref.1, f32[768,128]{1,0:T(8,128)} %long_convolutions.1.landed_ref), custom_call_target="tpu_custom_call" | custom-call | tf_op jit(solution)/shard_map/gate_gradients/pallas_call | solution.py:263

commit v2 on v1

--- a/solution.py
+++ b/solution.py
@@ -42,7 +42,7 @@
     peers = n_ctx * n_merge
     my_ctx = lax.axis_index("ctx")
     my_chan = lax.axis_index("chan") if n_merge > 1 else 0
-    me = my_ctx * n_merge + my_chan
+    me = my_chan * n_ctx + my_ctx
 
     offsets = [(c, j) for c in range(n_ctx) for j in range(n_merge) if (c, j) != (0, 0)]
     offsets.sort(key=lambda o: (abs(o[0] - n_ctx // 2), o))
@@ -51,7 +51,7 @@
         ctx = (my_ctx + c) % n_ctx
         chan = (my_chan + j) % n_merge if n_merge > 1 else 0
         ident = {"ctx": ctx, "chan": chan} if n_merge > 1 else {"ctx": ctx}
-        others.append((j == 0, ctx, chan, ctx * n_merge + chan, ident))
+        others.append((j == 0, ctx, chan, chan * n_ctx + ctx, ident))
 
     barrier = pltpu.get_barrier_semaphore()
     for _, _, _, _, ident in others:
@@ -145,16 +145,14 @@
                     s_land[at - 1 : at, :], s_land[at : at + 1, :]
                 )
 
-    def send_result(src_of, a):
-        for _, ctx, chan, peer, ident in others:
-            remote(src_of(ctx, chan), rows_at(landed_ref, (me * 3 + a) * tiles, tiles), 3 + a, ident).start()
-        own = pltpu.make_async_copy(
-            src_of(my_ctx, my_chan), rows_at(landed_ref, (me * 3 + a) * tiles, tiles), own_sem.at[a]
-        )
+    def share(src_of, to, n, peer_list):
+        for _, ctx, chan, peer, ident in peer_list:
+            remote(src_of(ctx, chan), rows_at(landed_ref, to, tiles), n, ident).start()
+        own = pltpu.make_async_copy(src_of(my_ctx, my_chan), rows_at(landed_ref, to, tiles), own_sem.at[n - 3])
         own.start()
         return own
 
-    owns = [send_result(lambda ctx, chan: rows_at(conv, chan * blocks + ctx * tiles, tiles), 0)]
+    conv_own = share(lambda ctx, chan: rows_at(conv, chan * blocks + ctx * tiles, tiles), me * 2 * tiles, 3, others)
 
     whole(c_stage, 2, peers - 1).wait_recv()
     for ch in range(n_merge):
@@ -162,6 +160,18 @@
         for dd in range(STEPS):
             at = ch * span + dd
             c_lhs[ch, :, dd * LANES : (dd + 1) * LANES] = c_pad[at : at + blocks, :].astype(BF16)
+
+    for g in range(blocks // STEPS):
+        n = blocks - g * STEPS
+        for ch in range(n_merge):
+            part = jnp.dot(c_lhs[ch, g * STEPS : blocks, :], band(1 + ch, g), preferred_element_type=F32)
+            corr[0:n, :] = part if g == 0 and ch == 0 else corr[0:n, :] + part
+    corr[...] = reverse(corr[...]) * scale
+    corr_rows = peers * 2 * tiles
+    corr_own = share(
+        lambda ctx, chan: rows_at(corr, ctx * tiles, tiles),
+        corr_rows + my_chan * blocks + my_ctx * tiles, 4, [o for o in others if o[0]],
+    )
 
     for g in range(blocks // STEPS):
         n = blocks - g * STEPS
@@ -172,37 +182,42 @@
             rows = slice(ch * blocks, ch * blocks + n)
             back[rows, :] = part if g == 0 else back[rows, :] + part
     back[...] = reverse(back[...])
-    owns.append(send_result(lambda ctx, chan: rows_at(back, chan * blocks + ctx * tiles, tiles), 1))
-
-    for g in range(blocks // STEPS):
-        n = blocks - g * STEPS
-        for ch in range(n_merge):
-            part = jnp.dot(c_lhs[ch, g * STEPS : blocks, :], band(1 + ch, g), preferred_element_type=F32)
-            corr[0:n, :] = part if g == 0 and ch == 0 else corr[0:n, :] + part
-    corr[...] = reverse(corr[...]) * scale
-    owns.append(send_result(lambda ctx, chan: rows_at(corr, ctx * tiles, tiles), 2))
+    back_own = share(
+        lambda ctx, chan: rows_at(back, chan * blocks + ctx * tiles, tiles), (me * 2 + 1) * tiles, 5, others
+    )
+
+    corr_own.wait()
+    whole(f_stage, 4, n_ctx - 1).wait_recv()
+    held = rows_at(landed_ref, corr_rows + my_chan * blocks, blocks)
+    for j in range(1, n_merge):
+        remote(held, held, 6, {"ctx": my_ctx, "chan": (my_chan + j) % n_merge}).start()
 
     whole(f_stage, 0, n_ctx - 1).wait_send()
     whole(s_stage, 1, peers - 1).wait_send()
     whole(c_stage, 2, peers - 1).wait_send()
-    for a in range(3):
-        owns[a].wait()
-        whole(s_stage, 3 + a, peers - 1).wait_send()
-        whole(s_stage, 3 + a, peers - 1).wait_recv()
+    conv_own.wait()
+    back_own.wait()
+    whole(s_stage, 3, peers - 1).wait_send()
+    whole(f_stage, 4, n_ctx - 1).wait_send()
+    whole(s_stage, 5, peers - 1).wait_send()
+    whole(s_stage, 3, peers - 1).wait_recv()
+    if n_merge > 1:
+        whole(s_stage, 6, (n_merge - 1) * n_ctx).wait_send()
+        whole(s_stage, 6, (n_merge - 1) * n_ctx).wait_recv()
+    whole(s_stage, 5, peers - 1).wait_recv()
 
 
 def gate_kernel(go_ref, k_ref, v_ref, landed_ref, dq_ref, dk_ref, dv_ref, df_ref):
     rows, width = go_ref.shape
     tiles = width // LANES
-    size = 3 * tiles
     for k in range(tiles):
         cols = slice(k * LANES, (k + 1) * LANES)
-        conv = landed_ref[pl.ds(k, rows, stride=size), :]
-        back = landed_ref[pl.ds(tiles + k, rows, stride=size), :]
+        conv = landed_ref[pl.ds(k, rows, stride=2 * tiles), :]
+        back = landed_ref[pl.ds(tiles + k, rows, stride=2 * tiles), :]
         dq_ref[:, cols] = (go_ref[:, cols].astype(F32) * conv).astype(BF16)
         dk_ref[:, cols] = (back * v_ref[:, cols].astype(F32)).astype(BF16)
         dv_ref[:, cols] = (back * k_ref[:, cols].astype(F32)).astype(BF16)
-        df_ref[:, cols] = landed_ref[pl.ds(2 * tiles + k, rows, stride=size), :]
+        df_ref[:, cols] = landed_ref[pl.ds(rows * 2 * tiles + k, rows, stride=tiles), :]
 
 
 def vmem(count):
@@ -251,8 +266,8 @@
             buffer(n_merge * blocks, LANES),
             buffer(n_merge * blocks, LANES),
             buffer(blocks, LANES),
-            dma((6,)),
-            dma((6,)),
+            dma((7,)),
+            dma((7,)),
             dma((3,)),
         ],
         compiler_params=pltpu.CompilerParams(

time: 31.5 us -> 31.6 us (level)
  no operation moved by 1% of the time
where the time goes in v2:
time: 31.6 us; the launch traced here: 31.5 us
  Pallas kernels  30.8 us (97%)
  between operations  0.64 us (2%)
    pallas_call x1, Pallas kernels, local(): pl.pallas_call(functools.partial(convolve_kernel, n_ctx, n_merge, scale),...  28.9 us
    pallas_call x1, Pallas kernels, local(): pl.pallas_call(gate_kernel, out_shape=(jax.ShapeDtypeStruct((rows, width)...  1.93 us

profile of v2, /device:TPU:0, one launch (start us, length us, event | category | flops | bytes accessed | tf_op | source)
XLA Modules:
  0.0 31.5 jit_solution(14885721938224259763)
XLA Ops:
  0.6 28.9 %long_convolutions.1.landed_ref = f32[768,128]{1,0:T(8,128)} custom-call(bf16[32,1024]{1,0:T(8,128)(2,1)} %go_ref.1, bf16[32,1024]{1,0:T(8,128)(2,1)} %q_hbm.1, bf16[32,1024]{1,0:T(8,128)(2,1)} %k_ref.1, bf16[32,1024]{1,0:T(8,128)(2,1)} %v_ref.1, f32[32,1024]{1,0:T(8,128)} %f_hbm.1), custom_call_target="tpu_custom_call" | custom-call | tf_op jit(solution)/shard_map/long_convolutions/pallas_call | solution.py:244
  29.5 1.9 %gate_gradients.1 = (bf16[32,1024]{1,0:T(8,128)(2,1)}, bf16[32,1024]{1,0:T(8,128)(2,1)}, bf16[32,1024]{1,0:T(8,128)(2,1)}, f32[32,1024]{1,0:T(8,128)}) custom-call(bf16[32,1024]{1,0:T(8,128)(2,1)} %go_ref.1, bf16[32,1024]{1,0:T(8,128)(2,1)} %k_ref.1, bf16[32,1024]{1,0:T(8,128)(2,1)} %v_ref.1, f32[768,128]{1,0:T(8,128)} %long_convolutions.1.landed_ref), custom_call_target="tpu_custom_call" | custom-call | tf_op jit(solution)/shard_map/gate_gradients/pallas_call | solution.py:278

commit v3 on v2

--- a/solution.py
+++ b/solution.py
@@ -97,36 +97,50 @@
         s_land[ch * span : ch * span + STEPS, :] = jnp.zeros((STEPS, LANES), F32)
         c_pad[ch * span + blocks : (ch + 1) * span, :] = jnp.zeros((STEPS, LANES), F32)
 
-    lane = lax.broadcasted_iota(jnp.int32, (LANES, LANES), 1)
-    row = lax.broadcasted_iota(jnp.int32, (LANES, LANES), 0)
-    flip = (lane + row == LANES - 1).astype(F32)
-    current = lane < LANES - row
+    flip = (
+        lax.broadcasted_iota(jnp.int32, (LANES, LANES), 0) + lax.broadcasted_iota(jnp.int32, (LANES, LANES), 1)
+        == LANES - 1
+    ).astype(BF16)
+    lane = lax.broadcasted_iota(jnp.int32, (8, LANES), 1)
+    first_rows = lane < LANES - lax.broadcasted_iota(jnp.int32, (8, LANES), 0)
 
     def reverse(values):
-        return jnp.dot(values, flip, precision=lax.Precision.HIGHEST, preferred_element_type=F32)
+        high = values.astype(BF16)
+        out = jnp.dot(high, flip, preferred_element_type=F32)
+        if values.dtype == F32:
+            low = (values - high.astype(F32)).astype(BF16)
+            out = out + jnp.dot(low, flip, preferred_element_type=F32)
+        return out
 
     def skew(before, now):
-        picked = jnp.where(
-            current, jnp.broadcast_to(now, (LANES, LANES)), jnp.broadcast_to(before, (LANES, LANES))
-        )
-        return pltpu.roll(picked, 0, 1, stride=1, stride_axis=0).astype(BF16)
+        picked = jnp.where(first_rows, jnp.broadcast_to(now, (8, LANES)), jnp.broadcast_to(before, (8, LANES)))
+        return pltpu.roll(picked, 0, 1, stride=1, stride_axis=0)
+
+    def tile(left, here):
+        parts = [here]
+        for shift in range(8, LANES, 8):
+            parts.append(pltpu.roll(jnp.where(lane < LANES - shift, here, left), shift, 1))
+        return jnp.concatenate(parts, axis=0).astype(BF16)
 
     whole(f_stage, 0, n_ctx - 1).wait_recv()
 
-    def build(src, before):
+    def build(src, carry):
+        before, left = carry
         rows = f_land[pl.ds(pl.multiple_of(src * tiles, 8), tiles), :]
         for k in range(tiles):
             now = rows[k : k + 1, :]
-            toep[0, pl.ds(pl.multiple_of((src * tiles + k) * LANES, LANES), LANES), :] = skew(before, now)
-            before = now
-        return before
-
-    lax.fori_loop(0, n_ctx, build, jnp.zeros((1, LANES), F32))
+            here = skew(before, now)
+            toep[0, pl.ds(pl.multiple_of((src * tiles + k) * LANES, LANES), LANES), :] = tile(left, here)
+            before, left = now, here
+        return before, left
+
+    lax.fori_loop(0, n_ctx, build, (jnp.zeros((1, LANES), F32), jnp.zeros((8, LANES), F32)))
     whole(s_stage, 1, peers - 1).wait_recv()
     for ch in range(n_merge):
         for dd in range(STEPS):
             at = ch * span + STEPS - dd
             s_lhs[ch, :, dd * LANES : (dd + 1) * LANES] = s_land[at : at + blocks, :].astype(BF16)
+    lefts = [jnp.zeros((8, LANES), F32)] * n_merge
 
     def band(n, g):
         return toep[n, g * DEPTH : (g + 1) * DEPTH, :]
@@ -141,9 +155,9 @@
             conv[rows, :] = part if g == 0 else conv[rows, :] + part
             for block in range(g * STEPS, (g + 1) * STEPS):
                 at = ch * span + STEPS + block
-                toep[1 + ch, block * LANES : (block + 1) * LANES, :] = skew(
-                    s_land[at - 1 : at, :], s_land[at : at + 1, :]
-                )
+                here = skew(s_land[at - 1 : at, :], s_land[at : at + 1, :])
+                toep[1 + ch, block * LANES : (block + 1) * LANES, :] = tile(lefts[ch], here)
+                lefts[ch] = here
 
     def share(src_of, to, n, peer_list):
         for _, ctx, chan, peer, ident in peer_list:
@@ -156,7 +170,7 @@
 
     whole(c_stage, 2, peers - 1).wait_recv()
     for ch in range(n_merge):
-        c_pad[ch * span : ch * span + blocks, :] = reverse(c_land[ch * blocks : (ch + 1) * blocks, :])
+        c_pad[ch * span : ch * span + blocks, :] = reverse(c_land[ch * blocks : (ch + 1) * blocks, :].astype(BF16))
         for dd in range(STEPS):
             at = ch * span + dd
             c_lhs[ch, :, dd * LANES : (dd + 1) * LANES] = c_pad[at : at + blocks, :].astype(BF16)

time: 31.6 us -> 38.6 us (1.22)
  Pallas kernels: 30.8 us -> 37.8 us
    pallas_call x1, Pallas kernels: 28.9 us -> 35.9 us  [local(): pl.pallas_call(functools.partial(convolve_kernel, n_ctx, n_merge, scale),...]
where the time goes in v3:
time: 38.6 us; the launch traced here: 38.5 us
  Pallas kernels  37.8 us (98%)
  between operations  0.64 us (2%)
    pallas_call x1, Pallas kernels, local(): pl.pallas_call(functools.partial(convolve_kernel, n_ctx, n_merge, scale),...  35.9 us
    pallas_call x1, Pallas kernels, local(): pl.pallas_call(gate_kernel, out_shape=(jax.ShapeDtypeStruct((rows, width)...  1.93 us

profile of v3, /device:TPU:0, one launch (start us, length us, event | category | flops | bytes accessed | tf_op | source)
XLA Modules:
  0.0 38.5 jit_solution(9176365774907169564)
XLA Ops:
  0.6 35.9 %long_convolutions.1.landed_ref = f32[768,128]{1,0:T(8,128)} custom-call(bf16[32,1024]{1,0:T(8,128)(2,1)} %go_ref.1, bf16[32,1024]{1,0:T(8,128)(2,1)} %q_hbm.1, bf16[32,1024]{1,0:T(8,128)(2,1)} %k_ref.1, bf16[32,1024]{1,0:T(8,128)(2,1)} %v_ref.1, f32[32,1024]{1,0:T(8,128)} %f_hbm.1), custom_call_target="tpu_custom_call" | custom-call | tf_op jit(solution)/shard_map/long_convolutions/pallas_call | solution.py:258
  36.5 1.9 %gate_gradients.1 = (bf16[32,1024]{1,0:T(8,128)(2,1)}, bf16[32,1024]{1,0:T(8,128)(2,1)}, bf16[32,1024]{1,0:T(8,128)(2,1)}, f32[32,1024]{1,0:T(8,128)}) custom-call(bf16[32,1024]{1,0:T(8,128)(2,1)} %go_ref.1, bf16[32,1024]{1,0:T(8,128)(2,1)} %k_ref.1, bf16[32,1024]{1,0:T(8,128)(2,1)} %v_ref.1, f32[768,128]{1,0:T(8,128)} %long_convolutions.1.landed_ref), custom_call_target="tpu_custom_call" | custom-call | tf_op jit(solution)/shard_map/gate_gradients/pallas_call | solution.py:292

commit v4 on v2

--- a/solution.py
+++ b/solution.py
@@ -26,7 +26,7 @@
 
 
 def convolve_kernel(n_ctx, n_merge, scale, go_hbm, q_hbm, k_hbm, v_hbm, f_hbm, landed_ref,
-                    go_ref, q_ref, k_ref, v_ref, f_ref, load_sem, f_stage, s_stage, c_stage, f_land, s_land, c_land, c_pad, s_lhs, c_lhs, toep,
+                    go_ref, q_ref, k_ref, v_ref, f_ref, load_sem, f_stage, s_stage, c_stage, f_land, s_land, c_land, c_pad, s_lhs, c_lhs, toep, gram, partial,
                     conv, back, corr, send_sem, recv_sem, own_sem):
     loads = [
         pltpu.make_async_copy(src, dst, load_sem.at[n])
@@ -93,17 +93,23 @@
     f_land[pl.ds(pl.multiple_of(my_ctx * tiles, 8), tiles), :] = f_stage[mine, :]
     s_land[pl.ds(pl.multiple_of(my_chan * span + STEPS + my_ctx * tiles, 8), tiles), :] = s_stage[mine, :]
     c_land[pl.ds(pl.multiple_of(my_chan * blocks + my_ctx * tiles, 8), tiles), :] = c_stage[mine, :]
+    gram[:, blocks * LANES : (blocks + 1) * LANES] = jnp.zeros((LANES, LANES), F32)
     for ch in range(n_merge):
         s_land[ch * span : ch * span + STEPS, :] = jnp.zeros((STEPS, LANES), F32)
         c_pad[ch * span + blocks : (ch + 1) * span, :] = jnp.zeros((STEPS, LANES), F32)
 
     lane = lax.broadcasted_iota(jnp.int32, (LANES, LANES), 1)
     row = lax.broadcasted_iota(jnp.int32, (LANES, LANES), 0)
-    flip = (lane + row == LANES - 1).astype(F32)
+    flip = (lane + row == LANES - 1).astype(BF16)
     current = lane < LANES - row
 
     def reverse(values):
-        return jnp.dot(values, flip, precision=lax.Precision.HIGHEST, preferred_element_type=F32)
+        high = values.astype(BF16)
+        out = jnp.dot(high, flip, preferred_element_type=F32)
+        if values.dtype == F32:
+            low = (values - high.astype(F32)).astype(BF16)
+            out = out + jnp.dot(low, flip, preferred_element_type=F32)
+        return out
 
     def skew(before, now):
         picked = jnp.where(
@@ -117,33 +123,30 @@
         rows = f_land[pl.ds(pl.multiple_of(src * tiles, 8), tiles), :]
         for k in range(tiles):
             now = rows[k : k + 1, :]
-            toep[0, pl.ds(pl.multiple_of((src * tiles + k) * LANES, LANES), LANES), :] = skew(before, now)
+            toep[pl.ds(pl.multiple_of((src * tiles + k) * LANES, LANES), LANES), :] = skew(before, now)
             before = now
         return before
 
     lax.fori_loop(0, n_ctx, build, jnp.zeros((1, LANES), F32))
     whole(s_stage, 1, peers - 1).wait_recv()
+    ahead = blocks - STEPS
     for ch in range(n_merge):
+        s_lhs[ch, 0:ahead, :] = jnp.zeros((ahead, DEPTH), BF16)
         for dd in range(STEPS):
             at = ch * span + STEPS - dd
-            s_lhs[ch, :, dd * LANES : (dd + 1) * LANES] = s_land[at : at + blocks, :].astype(BF16)
-
-    def band(n, g):
-        return toep[n, g * DEPTH : (g + 1) * DEPTH, :]
+            s_lhs[ch, ahead : ahead + blocks, dd * LANES : (dd + 1) * LANES] = s_land[at : at + blocks, :].astype(BF16)
+
+    def band(g):
+        return toep[g * DEPTH : (g + 1) * DEPTH, :]
 
     for g in range(blocks // STEPS):
         n = blocks - g * STEPS
-        lhs = jnp.concatenate([s_lhs[ch, 0:n, :] for ch in range(n_merge)], axis=0)
-        prod = jnp.dot(lhs, band(0, g), preferred_element_type=F32)
+        lhs = jnp.concatenate([s_lhs[ch, ahead : ahead + n, :] for ch in range(n_merge)], axis=0)
+        prod = jnp.dot(lhs, band(g), preferred_element_type=F32)
         for ch in range(n_merge):
             part = prod[ch * n : (ch + 1) * n]
             rows = slice(ch * blocks + g * STEPS, (ch + 1) * blocks)
             conv[rows, :] = part if g == 0 else conv[rows, :] + part
-            for block in range(g * STEPS, (g + 1) * STEPS):
-                at = ch * span + STEPS + block
-                toep[1 + ch, block * LANES : (block + 1) * LANES, :] = skew(
-                    s_land[at - 1 : at, :], s_land[at : at + 1, :]
-                )
 
     def share(src_of, to, n, peer_list):
         for _, ctx, chan, peer, ident in peer_list:
@@ -161,50 +164,47 @@
             at = ch * span + dd
             c_lhs[ch, :, dd * LANES : (dd + 1) * LANES] = c_pad[at : at + blocks, :].astype(BF16)
 
+    turned = jnp.concatenate(
+        [c_pad[ch * span : ch * span + blocks, :].T for ch in range(n_merge)], axis=1
+    ).astype(BF16)
     for g in range(blocks // STEPS):
-        n = blocks - g * STEPS
-        for ch in range(n_merge):
-            part = jnp.dot(c_lhs[ch, g * STEPS : blocks, :], band(1 + ch, g), preferred_element_type=F32)
-            corr[0:n, :] = part if g == 0 and ch == 0 else corr[0:n, :] + part
-    corr[...] = reverse(corr[...]) * scale
-    corr_rows = peers * 2 * tiles
-    corr_own = share(
-        lambda ctx, chan: rows_at(corr, ctx * tiles, tiles),
-        corr_rows + my_chan * blocks + my_ctx * tiles, 4, [o for o in others if o[0]],
-    )
+        at = ahead - g * STEPS
+        rhs = jnp.concatenate([s_lhs[ch, at : at + blocks, :] for ch in range(n_merge)], axis=0)
+        gram[:, g * DEPTH : (g + 1) * DEPTH] = jnp.dot(turned, rhs, preferred_element_type=F32)
 
     for g in range(blocks // STEPS):
         n = blocks - g * STEPS
         lhs = jnp.concatenate([c_lhs[ch, g * STEPS : blocks, :] for ch in range(n_merge)], axis=0)
-        prod = jnp.dot(lhs, band(0, g), preferred_element_type=F32)
+        prod = jnp.dot(lhs, band(g), preferred_element_type=F32)
         for ch in range(n_merge):
             part = prod[ch * n : (ch + 1) * n]
             rows = slice(ch * blocks, ch * blocks + n)
             back[rows, :] = part if g == 0 else back[rows, :] + part
+        for e in range(g * STEPS, (g + 1) * STEPS):
+            here = gram[:, e * LANES : (e + 1) * LANES]
+            later = gram[:, (e + 1) * LANES : (e + 2) * LANES]
+            turn = pltpu.roll(jnp.where(current, here, later), 0, 1, stride=1, stride_axis=0)
+            partial[e * 8 : (e + 1) * 8, :] = jnp.sum(turn.reshape(LANES // 8, 8, LANES), axis=0)
     back[...] = reverse(back[...])
     back_own = share(
         lambda ctx, chan: rows_at(back, chan * blocks + ctx * tiles, tiles), (me * 2 + 1) * tiles, 5, others
     )
-
-    corr_own.wait()
-    whole(f_stage, 4, n_ctx - 1).wait_recv()
-    held = rows_at(landed_ref, corr_rows + my_chan * blocks, blocks)
-    for j in range(1, n_merge):
-        remote(held, held, 6, {"ctx": my_ctx, "chan": (my_chan + j) % n_merge}).start()
+    total = partial[pl.ds(0, blocks, stride=8), :]
+    for k in range(1, 8):
+        total = total + partial[pl.ds(k, blocks, stride=8), :]
+    corr[...] = reverse(total) * scale
+    corr_own = share(
+        lambda ctx, chan: rows_at(corr, ctx * tiles, tiles), peers * 2 * tiles + me * tiles, 4, others
+    )
 
     whole(f_stage, 0, n_ctx - 1).wait_send()
     whole(s_stage, 1, peers - 1).wait_send()
     whole(c_stage, 2, peers - 1).wait_send()
-    conv_own.wait()
-    back_own.wait()
-    whole(s_stage, 3, peers - 1).wait_send()
-    whole(f_stage, 4, n_ctx - 1).wait_send()
-    whole(s_stage, 5, peers - 1).wait_send()
-    whole(s_stage, 3, peers - 1).wait_recv()
-    if n_merge > 1:
-        whole(s_stage, 6, (n_merge - 1) * n_ctx).wait_send()
-        whole(s_stage, 6, (n_merge - 1) * n_ctx).wait_recv()
-    whole(s_stage, 5, peers - 1).wait_recv()
+    for own in (conv_own, back_own, corr_own):
+        own.wait()
+    for n in (3, 5, 4):
+        whole(s_stage, n, peers - 1).wait_send()
+        whole(s_stage, n, peers - 1).wait_recv()
 
 
 def gate_kernel(go_ref, k_ref, v_ref, landed_ref, dq_ref, dk_ref, dv_ref, df_ref):
@@ -260,14 +260,16 @@
             buffer(n_merge * span, LANES),
             buffer(n_merge * blocks, LANES),
             buffer(n_merge * span, LANES),
+            buffer(n_merge, 2 * blocks - STEPS, DEPTH, dtype=BF16),
             buffer(n_merge, blocks, DEPTH, dtype=BF16),
-            buffer(n_merge, blocks, DEPTH, dtype=BF16),
-            buffer(1 + n_merge, blocks * LANES, LANES, dtype=BF16),
+            buffer(blocks * LANES, LANES, dtype=BF16),
+            buffer(LANES, (blocks + 1) * LANES),
+            buffer(blocks * 8, LANES),
             buffer(n_merge * blocks, LANES),
             buffer(n_merge * blocks, LANES),
             buffer(blocks, LANES),
-            dma((7,)),
-            dma((7,)),
+            dma((6,)),
+            dma((6,)),
             dma((3,)),
         ],
         compiler_params=pltpu.CompilerParams(

time: 31.6 us -> 31 us (0.981)
  Pallas kernels: 30.8 us -> 30.2 us
    pallas_call x1, Pallas kernels: 28.9 us -> 28.3 us  [local(): pl.pallas_call(functools.partial(convolve_kernel, n_ctx, n_merge, scale),...]
where the time goes in v4:
time: 31 us; the launch traced here: 30.9 us
  Pallas kernels  30.2 us (97%)
  between operations  0.64 us (2%)
    pallas_call x1, Pallas kernels, local(): pl.pallas_call(functools.partial(convolve_kernel, n_ctx, n_merge, scale),...  28.3 us
    pallas_call x1, Pallas kernels, local(): pl.pallas_call(gate_kernel, out_shape=(jax.ShapeDtypeStruct((rows, width)...  1.93 us

profile of v4, /device:TPU:0, one launch (start us, length us, event | category | flops | bytes accessed | tf_op | source)
XLA Modules:
  0.0 30.9 jit_solution(1215067899368737634)
XLA Ops:
  0.6 28.3 %long_convolutions.1.landed_ref = f32[768,128]{1,0:T(8,128)} custom-call(bf16[32,1024]{1,0:T(8,128)(2,1)} %go_ref.1, bf16[32,1024]{1,0:T(8,128)(2,1)} %q_hbm.1, bf16[32,1024]{1,0:T(8,128)(2,1)} %k_ref.1, bf16[32,1024]{1,0:T(8,128)(2,1)} %v_ref.1, f32[32,1024]{1,0:T(8,128)} %f_hbm.1), custom_call_target="tpu_custom_call" | custom-call | tf_op jit(solution)/shard_map/long_convolutions/pallas_call | solution.py:244
  28.9 1.9 %gate_gradients.1 = (bf16[32,1024]{1,0:T(8,128)(2,1)}, bf16[32,1024]{1,0:T(8,128)(2,1)}, bf16[32,1024]{1,0:T(8,128)(2,1)}, f32[32,1024]{1,0:T(8,128)}) custom-call(bf16[32,1024]{1,0:T(8,128)(2,1)} %go_ref.1, bf16[32,1024]{1,0:T(8,128)(2,1)} %k_ref.1, bf16[32,1024]{1,0:T(8,128)(2,1)} %v_ref.1, f32[768,128]{1,0:T(8,128)} %long_convolutions.1.landed_ref), custom_call_target="tpu_custom_call" | custom-call | tf_op jit(solution)/shard_map/gate_gradients/pallas_call | solution.py:280

commit v5 on v4

--- a/solution.py
+++ b/solution.py
@@ -72,6 +72,15 @@
     loads[1].wait()
     loads[2].wait()
     split_rows(k_ref[...].astype(F32) * v_ref[...].astype(F32), s_stage, tiles)
+    loads[3].wait()
+    loads[4].wait()
+    split_rows(go_ref[...].astype(F32) * q_ref[...].astype(F32), c_stage, tiles)
+    ahead = blocks - STEPS
+    gram[:, blocks * LANES : (blocks + 1) * LANES] = jnp.zeros((LANES, LANES), F32)
+    for ch in range(n_merge):
+        s_land[ch * span : ch * span + STEPS, :] = jnp.zeros((STEPS, LANES), F32)
+        c_pad[ch * span + blocks : (ch + 1) * span, :] = jnp.zeros((STEPS, LANES), F32)
+        s_lhs[ch, 0:ahead, :] = jnp.zeros((ahead, DEPTH), BF16)
     pl.semaphore_wait(barrier, peers - 1)
     for same, ctx, chan, peer, ident in others:
         if same:
@@ -81,9 +90,6 @@
             rows_at(s_stage, peer * tiles, tiles),
             rows_at(s_land, my_chan * span + STEPS + my_ctx * tiles, tiles), 1, ident,
         ).start()
-    loads[3].wait()
-    loads[4].wait()
-    split_rows(go_ref[...].astype(F32) * q_ref[...].astype(F32), c_stage, tiles)
     for _, ctx, chan, peer, ident in others:
         remote(
             rows_at(c_stage, peer * tiles, tiles),
@@ -93,11 +99,6 @@
     f_land[pl.ds(pl.multiple_of(my_ctx * tiles, 8), tiles), :] = f_stage[mine, :]
     s_land[pl.ds(pl.multiple_of(my_chan * span + STEPS + my_ctx * tiles, 8), tiles), :] = s_stage[mine, :]
     c_land[pl.ds(pl.multiple_of(my_chan * blocks + my_ctx * tiles, 8), tiles), :] = c_stage[mine, :]
-    gram[:, blocks * LANES : (blocks + 1) * LANES] = jnp.zeros((LANES, LANES), F32)
-    for ch in range(n_merge):
-        s_land[ch * span : ch * span + STEPS, :] = jnp.zeros((STEPS, LANES), F32)
-        c_pad[ch * span + blocks : (ch + 1) * span, :] = jnp.zeros((STEPS, LANES), F32)
-
     lane = lax.broadcasted_iota(jnp.int32, (LANES, LANES), 1)
     row = lax.broadcasted_iota(jnp.int32, (LANES, LANES), 0)
     flip = (lane + row == LANES - 1).astype(BF16)
@@ -129,9 +130,7 @@
 
     lax.fori_loop(0, n_ctx, build, jnp.zeros((1, LANES), F32))
     whole(s_stage, 1, peers - 1).wait_recv()
-    ahead = blocks - STEPS
     for ch in range(n_merge):
-        s_lhs[ch, 0:ahead, :] = jnp.zeros((ahead, DEPTH), BF16)
         for dd in range(STEPS):
             at = ch * span + STEPS - dd
             s_lhs[ch, ahead : ahead + blocks, dd * LANES : (dd + 1) * LANES] = s_land[at : at + blocks, :].astype(BF16)
@@ -164,14 +163,6 @@
             at = ch * span + dd
             c_lhs[ch, :, dd * LANES : (dd + 1) * LANES] = c_pad[at : at + blocks, :].astype(BF16)
 
-    turned = jnp.concatenate(
-        [c_pad[ch * span : ch * span + blocks, :].T for ch in range(n_merge)], axis=1
-    ).astype(BF16)
-    for g in range(blocks // STEPS):
-        at = ahead - g * STEPS
-        rhs = jnp.concatenate([s_lhs[ch, at : at + blocks, :] for ch in range(n_merge)], axis=0)
-        gram[:, g * DEPTH : (g + 1) * DEPTH] = jnp.dot(turned, rhs, preferred_element_type=F32)
-
     for g in range(blocks // STEPS):
         n = blocks - g * STEPS
         lhs = jnp.concatenate([c_lhs[ch, g * STEPS : blocks, :] for ch in range(n_merge)], axis=0)
@@ -180,15 +171,29 @@
             part = prod[ch * n : (ch + 1) * n]
             rows = slice(ch * blocks, ch * blocks + n)
             back[rows, :] = part if g == 0 else back[rows, :] + part
+    back[...] = reverse(back[...])
+    back_own = share(
+        lambda ctx, chan: rows_at(back, chan * blocks + ctx * tiles, tiles), (me * 2 + 1) * tiles, 5, others
+    )
+
+    turned = jnp.concatenate(
+        [c_pad[ch * span : ch * span + blocks, :].T for ch in range(n_merge)], axis=1
+    ).astype(BF16)
+
+    def diagonals(g):
         for e in range(g * STEPS, (g + 1) * STEPS):
             here = gram[:, e * LANES : (e + 1) * LANES]
             later = gram[:, (e + 1) * LANES : (e + 2) * LANES]
             turn = pltpu.roll(jnp.where(current, here, later), 0, 1, stride=1, stride_axis=0)
             partial[e * 8 : (e + 1) * 8, :] = jnp.sum(turn.reshape(LANES // 8, 8, LANES), axis=0)
-    back[...] = reverse(back[...])
-    back_own = share(
-        lambda ctx, chan: rows_at(back, chan * blocks + ctx * tiles, tiles), (me * 2 + 1) * tiles, 5, others
-    )
+
+    for g in range(blocks // STEPS):
+        at = ahead - g * STEPS
+        rhs = jnp.concatenate([s_lhs[ch, at : at + blocks, :] for ch in range(n_merge)], axis=0)
+        gram[:, g * DEPTH : (g + 1) * DEPTH] = jnp.dot(turned, rhs, preferred_element_type=F32)
+        if g > 0:
+            diagonals(g - 1)
+    diagonals(blocks // STEPS - 1)
     total = partial[pl.ds(0, blocks, stride=8), :]
     for k in range(1, 8):
         total = total + partial[pl.ds(k, blocks, stride=8), :]

time: 31 us -> 30.7 us (level)
    pallas_call x1, Pallas kernels: 28.3 us -> 27.9 us  [local(): pl.pallas_call(functools.partial(convolve_kernel, n_ctx, n_merge, scale),...]
where the time goes in v5:
time: 30.7 us; the launch traced here: 30.5 us
  Pallas kernels  29.9 us (97%)
  between operations  0.64 us (2%)
    pallas_call x1, Pallas kernels, local(): pl.pallas_call(functools.partial(convolve_kernel, n_ctx, n_merge, scale),...  27.9 us
    pallas_call x1, Pallas kernels, local(): pl.pallas_call(gate_kernel, out_shape=(jax.ShapeDtypeStruct((rows, width)...  1.93 us

profile of v5, /device:TPU:0, one launch (start us, length us, event | category | flops | bytes accessed | tf_op | source)
XLA Modules:
  0.0 30.5 jit_solution(14064054343949399401)
XLA Ops:
  0.6 27.9 %long_convolutions.1.landed_ref = f32[768,128]{1,0:T(8,128)} custom-call(bf16[32,1024]{1,0:T(8,128)(2,1)} %go_ref.1, bf16[32,1024]{1,0:T(8,128)(2,1)} %q_hbm.1, bf16[32,1024]{1,0:T(8,128)(2,1)} %k_ref.1, bf16[32,1024]{1,0:T(8,128)(2,1)} %v_ref.1, f32[32,1024]{1,0:T(8,128)} %f_hbm.1), custom_call_target="tpu_custom_call" | custom-call | tf_op jit(solution)/shard_map/long_convolutions/pallas_call | solution.py:249
  28.6 1.9 %gate_gradients.1 = (bf16[32,1024]{1,0:T(8,128)(2,1)}, bf16[32,1024]{1,0:T(8,128)(2,1)}, bf16[32,1024]{1,0:T(8,128)(2,1)}, f32[32,1024]{1,0:T(8,128)}) custom-call(bf16[32,1024]{1,0:T(8,128)(2,1)} %go_ref.1, bf16[32,1024]{1,0:T(8,128)(2,1)} %k_ref.1, bf16[32,1024]{1,0:T(8,128)(2,1)} %v_ref.1, f32[768,128]{1,0:T(8,128)} %long_convolutions.1.landed_ref), custom_call_target="tpu_custom_call" | custom-call | tf_op jit(solution)/shard_map/gate_gradients/pallas_call | solution.py:285

commit v6 on v5

--- a/solution.py
+++ b/solution.py
@@ -46,6 +46,8 @@
 
     offsets = [(c, j) for c in range(n_ctx) for j in range(n_merge) if (c, j) != (0, 0)]
     offsets.sort(key=lambda o: (abs(o[0] - n_ctx // 2), o))
+    half = (len(offsets) + 1) // 2
+    offsets = [o for k in range(half) for o in dict.fromkeys((offsets[k], offsets[len(offsets) - 1 - k]))]
     others = []
     for c, j in offsets:
         ctx = (my_ctx + c) % n_ctx

time: 30.7 us -> 29.8 us (0.971)
  Pallas kernels: 29.9 us -> 28.9 us
    pallas_call x1, Pallas kernels: 27.9 us -> 27 us  [local(): pl.pallas_call(functools.partial(convolve_kernel, n_ctx, n_merge, scale),...]
where the time goes in v6:
time: 29.8 us; the launch traced here: 29.6 us
  Pallas kernels  28.9 us (97%)
  between operations  0.64 us (2%)
    pallas_call x1, Pallas kernels, local(): pl.pallas_call(functools.partial(convolve_kernel, n_ctx, n_merge, scale),...  27 us
    pallas_call x1, Pallas kernels, local(): pl.pallas_call(gate_kernel, out_shape=(jax.ShapeDtypeStruct((rows, width)...  1.93 us

profile of v6, /device:TPU:0, one launch (start us, length us, event | category | flops | bytes accessed | tf_op | source)
XLA Modules:
  0.0 29.6 jit_solution(9904639796568224063)
XLA Ops:
  0.6 27.0 %long_convolutions.1.landed_ref = f32[768,128]{1,0:T(8,128)} custom-call(bf16[32,1024]{1,0:T(8,128)(2,1)} %go_ref.1, bf16[32,1024]{1,0:T(8,128)(2,1)} %q_hbm.1, bf16[32,1024]{1,0:T(8,128)(2,1)} %k_ref.1, bf16[32,1024]{1,0:T(8,128)(2,1)} %v_ref.1, f32[32,1024]{1,0:T(8,128)} %f_hbm.1), custom_call_target="tpu_custom_call" | custom-call | tf_op jit(solution)/shard_map/long_convolutions/pallas_call | solution.py:251
  27.6 1.9 %gate_gradients.1 = (bf16[32,1024]{1,0:T(8,128)(2,1)}, bf16[32,1024]{1,0:T(8,128)(2,1)}, bf16[32,1024]{1,0:T(8,128)(2,1)}, f32[32,1024]{1,0:T(8,128)}) custom-call(bf16[32,1024]{1,0:T(8,128)(2,1)} %go_ref.1, bf16[32,1024]{1,0:T(8,128)(2,1)} %k_ref.1, bf16[32,1024]{1,0:T(8,128)(2,1)} %v_ref.1, f32[768,128]{1,0:T(8,128)} %long_convolutions.1.landed_ref), custom_call_target="tpu_custom_call" | custom-call | tf_op jit(solution)/shard_map/gate_gradients/pallas_call | solution.py:287
